TPU v7x, 32 devices: a whole 2x2x4 slice. The times are simulated.
32 devices in a mesh: group: 2 (over y), tensor: 4 (over z), batch: 4 (over x, core).
Axes of the slice: x: 2, y: 2, z: 4, core: 2. Of those that a mesh axis runs over, the one named last changes fastest.
Arguments:
- hidden_input: bfloat16 [2, 512, 8192], P(None, ('group', 'batch'), 'tensor'), parts along dimension 1, may hold values from -6 to 6
- projection_weight: bfloat16 [8192, 8192], P('tensor', 'batch'), may hold values from -0.0625 to 0.0625
- adapter_down_rows: bfloat16 [128, 64, 8192], P('batch', None, 'tensor'), may hold values from -0.0625 to 0.0625
- adapter_up_rows: bfloat16 [128, 64, 8192], P('batch', None, 'tensor'), may hold values from -0.75 to 0.75
- adapter_row_map: int32 [256], P('group'), parts along dimension 0, may hold values from 0 to 127, as said below
- segment_index_rows: int32 [2, 8, 64], P(None, ('group', 'batch')), parts along dimension 1, may hold values from 0 to 3, never falling along the last dimension, each value on 1 to 32 neighbouring positions
- segment_adapter: int32 [2, 8, 4], P(None, 'group'), parts along dimension 1, may hold values from 0 to 127, as said below
Outputs:
- projected: bfloat16 [2, 512, 8192], P(None, ('group', 'batch'), 'tensor'), parts along dimension 1
There are 2 independent parts, one for each index of `group`. A program takes and returns all parts, laid end to end along the dimension named above; an argument that names none is the same for every part. Nothing has to cross between parts.
Inputs may be any that keep to these rules, and one draw needn't show every extreme that they name: A permutation: adapter a's factors are row adapter_row_map[a] of adapter_down_rows and adapter_up_rows, stored on index adapter_row_map[a] // 32 of batch. `segment_adapter`: within one step and one index of batch the 4 entries are different adapters; of them exactly 0 or 2 are stored on each index of batch, so at most 2 and this most is reached. `segment_index_rows`: never falling along a device's requests; every segment has at least one request.
All inputs are finite; a program needn't handle non-finite values.
Results may differ from a plain program's by a relative error of at most 0.012.
Values may be sent and summed in bfloat16 or wider, within the bound.
A program may use at most 192 MiB of HBM per device.

v0:
```python
import jax
import jax.numpy as jnp
from jax import lax
from jax.sharding import PartitionSpec as P

CAP = 2


def owned_slots(segment_adapter, adapter_row_map, stored_count, own_index):
    slot_count = segment_adapter.shape[-1]
    position = jnp.take(adapter_row_map, segment_adapter, axis=0)
    owned = position // stored_count == own_index
    local_index = position % stored_count
    rank = jnp.cumsum(owned.astype(jnp.int32), axis=-1) - 1
    picked = owned[..., None, :] & (rank[..., None, :] == jnp.arange(CAP)[:, None])
    slot = jnp.sum(jnp.where(picked, jnp.arange(slot_count), 0), axis=-1)
    local = jnp.sum(jnp.where(picked, local_index[..., None, :], 0), axis=-1)
    filled = jnp.any(picked, axis=-1)
    return slot, local, filled


def shards_general(
    hidden_input,
    projection_weight,
    adapter_down_rows,
    adapter_up_rows,
    adapter_row_map,
    segment_index_rows,
    segment_adapter,
):
    steps, req, _ = hidden_input.shape
    batch_count = lax.axis_size("batch")
    stored_count, rank_width, _ = adapter_down_rows.shape
    own_index = lax.axis_index("batch")
    hidden = lax.all_gather(hidden_input, "batch", axis=1, tiled=True)
    segments = lax.all_gather(segment_index_rows, "batch", axis=1, tiled=True)
    slot, local, filled = owned_slots(segment_adapter, adapter_row_map, stored_count, own_index)
    mask = (segments[..., None] == slot[:, :, None, :]) & filled[:, :, None, :]
    grouped = hidden.reshape(steps, batch_count, req, -1)
    down = jnp.take(adapter_down_rows, local, axis=0)
    shrink_all = jnp.einsum("sbrd,sbckd->sbrck", grouped, down, preferred_element_type=jnp.float32)
    shrink_part = jnp.sum(jnp.where(mask[..., None], shrink_all, 0.0), axis=3)
    shrink = lax.psum(shrink_part.astype(jnp.bfloat16), "tensor")
    base_part = jnp.einsum(
        "srd,do->sro", hidden, projection_weight, preferred_element_type=jnp.float32
    ).astype(jnp.bfloat16)
    base_rows = lax.all_to_all(base_part, "batch", split_axis=1, concat_axis=2, tiled=True)
    base = lax.psum_scatter(base_rows, "tensor", scatter_dimension=2, tiled=True)
    masked = jnp.where(mask[..., None], shrink[:, :, :, None, :], jnp.zeros((), jnp.bfloat16))
    masked = masked.reshape(steps, batch_count, req, CAP * rank_width)
    up = jnp.take(adapter_up_rows, local, axis=0)
    up = up.reshape(steps, batch_count, CAP * rank_width, -1)
    term = jnp.einsum("sbrm,sbmo->sbro", masked, up, preferred_element_type=jnp.float32)
    term = lax.psum_scatter(term.astype(jnp.bfloat16), "batch", scatter_dimension=1, tiled=False)
    return (base.astype(jnp.float32) + term.astype(jnp.float32)).astype(jnp.bfloat16)


def solution(mesh):
    in_specs = (
        P(None, ("group", "batch"), "tensor"),
        P("tensor", "batch"),
        P("batch", None, "tensor"),
        P("batch", None, "tensor"),
        P("group"),
        P(None, ("group", "batch"), None),
        P(None, "group", None),
    )
    out_specs = P(None, ("group", "batch"), "tensor")
    return jax.shard_map(
        shards_general, mesh=mesh, in_specs=in_specs, out_specs=out_specs, check_vma=False
    )
```

profile of v0, /device:TPU:6, one launch (start us, length us, event | category | flops | bytes accessed | tf_op | source)
XLA Modules:
  0.0 185.6 jit_solution(3598060935070301217)
XLA Ops:
  6.5 0.7 all-gather.2.cloned.1.call-update
  7.3 0.7 compare_select_fusion
  8.1 0.7 gather_fusion
  8.9 0.4 reduce_window_sum.11
  9.3 0.2 select_reduce_fusion
  9.5 0.1 reduce_or.9
  9.9 5.1 %all_gather.7 = s32[2,4,64]{2,0,1:T(2,128)S(1)} all-gather(s32[2,1,64]{2,0,1:T(2,128)S(1)} %bitcast.43), channel_id=1, replica_groups=mesh['group'=2,'tensor'=4,'batch'=4] {'batch'}, dimensions={1}, use_global_device_ids=true | all-gather | bytes 2560 | tf_op jit(solution)/shard_map/all_gather | solution.py:36
  15.2 0.1 copy.23
  15.3 6.8 %gather_fusion.1 = bf16[16,64,2048]{2,1,0:T(8,128)(2,1)} fusion(bf16[32,64,2048]{2,1,0:T(8,128)(2,1)} %param.11, s32[1024]{0:T(1024)S(1)} %pad_clamp_fusion), kind=kCustom, calls=%fused_computation.clone | custom fusion | bytes 8388672 | tf_op jit(solution)/shard_map/jit(_take)/gather | solution.py:40
  22.1 6.2 %gather_fusion.2 = bf16[16,64,2048]{2,1,0:T(8,128)(2,1)} fusion(bf16[32,64,2048]{2,1,0:T(8,128)(2,1)} %param.12, s32[1024]{0:T(1024)S(1)} %pad_clamp_fusion), kind=kCustom, calls=%fused_computation.1.clone | custom fusion | bytes 8388672 | tf_op jit(solution)/shard_map/jit(_take)/gather | solution.py:51
  28.4 4.6 %broadcast_select_fusion = bf16[2,4,2,64,2048]{4,3,2,1,0:T(8,128)(2,1)} fusion(bf16[2,4,2,64,2048]{4,3,2,1,0:T(8,128)(2,1)} %bitcast.39, pred[2,4,2]{2,1,0:T(4,128)(4,1)S(1)} %copy.23), kind=kLoop, calls=%fused_computation.7 | loop fusion | flops 2097152 | bytes 8388624 | tf_op jit(solution)/shard_map/jit(_take)/select_n | solution.py:51
  33.0 4.9 %fusion.15 = bf16[2,4,64,64]{2,3,1,0:T(8,128)(2,1)} fusion(bf16[2,4,64,2048,1]{3,2,4,1,0:T(8,128)(2,1)} %bitcast.44, bf16[2,4,2,64,2048]{4,3,2,1,0:T(8,128)(2,1)} %bitcast.41, pred[2,4,2]{2,1,0:T(4,128)(4,1)S(1)} %copy.23, pred[2,4,64,2]{2,3,1,0:T(4,128)(4,1)S(1)} %compare_and_fusion), kind=kOutput, calls=%fused_computation.14 | convolution fusion | flops 270630912 | bytes 6358032 | tf_op jit(solution)/shard_map/sbrd,sbckd->sbrck/dot_general | solution.py:41
  37.9 8.5 %fusion.5 = bf16[2,256,2048]{2,1,0:T(8,128)(2,1)S(1)} fusion(bf16[2,256,2048]{2,1,0:T(8,128)(2,1)} %all-gather.2.cloned.1.call-done, bf16[2048,2048]{1,0:T(8,128)(2,1)} %param.10), kind=kOutput, calls=%fused_computation.9 | convolution fusion | flops 4296015872 | bytes 12582912 | tf_op jit(solution)/shard_map/srd,do->sro/dot_general | solution.py:44
  46.4 3.5 %copy.17 = bf16[2,256,2048]{2,0,1:T(2,128)(2,1)} copy(bf16[2,256,2048]{2,1,0:T(8,128)(2,1)S(1)} %fusion.5) | data formatting | bytes 4194304 | tf_op jit(solution)/shard_map/convert_element_type | solution.py:46
  50.0 4.1 %all-to-all-start = ((bf16[2,256,2048]{2,0,1:T(2,128)(2,1)}), bf16[2,256,2048]{2,0,1:T(2,128)(2,1)S(1)}, u32[]{:S(2)}, u32[]{:S(2)}) async-start(bf16[2,256,2048]{2,0,1:T(2,128)(2,1)} %copy.17), calls=%async_computation | async-start | bytes 4194304 | tf_op jit(solution)/shard_map/all_to_all | solution.py:47
  54.0 19.6 %all-reduce.4.cloned.1.call-done = bf16[2,4,64,64]{2,3,1,0:T(8,128)(2,1)} async-done(((bf16[2,4,64,64]{2,3,1,0:T(8,128)(2,1)}), bf16[2,4,64,64]{2,3,1,0:T(8,128)(2,1)}) %all-reduce.4.cloned.1.call-update) | async-done | bytes 65552 | tf_op jit(solution)/shard_map/psum | solution.py:43
  73.7 0.9 broadcast_select_fusion.1
  74.6 4.3 %convolution_convert_fusion = bf16[2,4,64,2048]{3,2,1,0:T(8,128)(2,1)} fusion(bf16[2,4,64,128]{2,3,1,0:T(8,128)(2,1)S(1)} %bitcast.42, bf16[2,4,128,2048]{3,2,1,0:T(8,128)(2,1)} %bitcast.38), kind=kOutput, calls=%fused_computation.10 | convolution fusion | flops 269484032 | bytes 6422528 | tf_op jit(solution)/shard_map/sbrm,sbmo->sbro/dot_general | solution.py:53
  79.0 3.0 %copy.18 = bf16[2,64,4,2048]{3,2,1,0:T(4,128)(2,1)} copy(bf16[2,64,4,2048]{3,0,1,2:T(2,128)(2,1)S(1)} %bitcast.40) | data formatting | bytes 4194304 | tf_op jit(solution)/shard_map/all_to_all | solution.py:47
  82.0 4.5 %all_to_all.16 = bf16[2,64,8192]{2,1,0:T(8,128)(2,1)} reshape(bf16[2,64,4,2048]{3,2,1,0:T(4,128)(2,1)} %copy.18) | data formatting | bytes 4194304 | tf_op jit(solution)/shard_map/all_to_all | solution.py:47
  86.5 0.7 dynamic-slice
  87.2 42.1 %all-reduce.6.cloned.1.call-done = bf16[2,4,64,2048]{3,2,1,0:T(8,128)(2,1)} async-done(((bf16[2,4,64,2048]{3,2,1,0:T(8,128)(2,1)}), bf16[2,4,64,2048]{3,2,1,0:T(8,128)(2,1)}) %all-reduce.6.cloned.1.call-update) | async-done | bytes 2097168
  129.3 47.0 %reduce-scatter.5.cloned.1.call-done = bf16[2,64,2048]{2,1,0:T(8,128)(2,1)} async-done(((bf16[2,64,8192]{2,1,0:T(8,128)(2,1)}), bf16[2,64,2048]{2,1,0:T(8,128)(2,1)}) %reduce-scatter.5.cloned.1.call-update) | async-done | bytes 524304 | tf_op jit(solution)/shard_map/reduce_scatter | solution.py:48
  176.3 2.8 %fusion.18 = bf16[2,64,2048]{2,1,0:T(8,128)(2,1)} fusion(bf16[2,64,2048]{2,1,0:T(8,128)(2,1)} %reduce-scatter.5.cloned.1.call-done, bf16[2,4,64,2048]{3,2,1,0:T(8,128)(2,1)} %all-reduce.6.cloned.1.call-done, u32[]{:T(128)} %bitcast.22), kind=kLoop, calls=%fused_computation.16 | loop fusion | flops 1048576 | bytes 1572868 | tf_op jit(solution)/shard_map/convert_element_type | solution.py:55
  (31 shorter events, 0.9 us)
Async XLA Ops:
  6.5 1.6 copy-start
  6.5 2.4 %copy-start.1 = (s32[2,4,4]{2,1,0:T(4,128)S(1)}, s32[2,4,4]{2,1,0:T(4,128)}, u32[]{:S(2)}) copy-start(s32[2,4,4]{2,1,0:T(4,128)} %param.15) | copy-start | bytes 388
  6.5 3.4 %copy-start.2 = (s32[2,1,64]{2,1,0:T(1,128)S(1)}, s32[2,1,64]{2,1,0:T(1,128)}, u32[]{:S(2)}) copy-start(s32[2,1,64]{2,1,0:T(1,128)} %param.14) | copy-start | bytes 1540
  6.5 26.5 %all-gather.2.cloned.1.call-start = ((), (), s32[]{:S(2)}) async-start(), calls=%async_computation.2 | async-start | bytes 2621440 | tf_op jit(solution)/shard_map/all_gather | solution.py:35
  7.3 66.4 %all-reduce.4.cloned.1.call-start = ((), (), s32[]{:S(2)}) async-start(), calls=%async_computation.4 | async-start | bytes 262144 | tf_op jit(solution)/shard_map/psum | solution.py:43
  50.0 29.0 %all-to-all-start = ((bf16[2,256,2048]{2,0,1:T(2,128)(2,1)}), bf16[2,256,2048]{2,0,1:T(2,128)(2,1)S(1)}, u32[]{:S(2)}, u32[]{:S(2)}) async-start(bf16[2,256,2048]{2,0,1:T(2,128)(2,1)} %copy.17), calls=%async_computation | async-start | bytes 4194304 | tf_op jit(solution)/shard_map/all_to_all | solution.py:47
  54.0 75.3 %all-reduce.6.cloned.1.call-start = ((), (), s32[]{:S(2)}) async-start(), calls=%async_computation.5 | async-start | bytes 4194304
  78.9 97.3 %reduce-scatter.5.cloned.1.call-start = ((), (), s32[]{:S(2)}) async-start(), calls=%async_computation.3 | async-start | bytes 2621440 | tf_op jit(solution)/shard_map/reduce_scatter | solution.py:48
  82.0 4.6 %copy-start.3 = (u32[32]{0:T(128)S(1)}, u32[32]{0:T(128)}, u32[]{:S(2)}) copy-start(u32[32]{0:T(128)} %constant.72) | copy-start | bytes 388
Sparse Core Ops, SparseCore 0:
  8.9 22.8 all-gather.1
  38.0 35.5 all-reduce.3
  79.0 50.2 all-reduce.5
  131.4 44.7 reduce-scatter.4
where the time goes:
time: 188 us; the launch traced here: 186 us
  waiting for transfers between devices  109 us (58%)
  local copies, waits for them, and re-layouts  26.1 us (14%)
  matrix products  17.7 us (9%)
  between operations  13.2 us (7%)
  other arithmetic  9.92 us (5%)
  blocking collectives  5.07 us (3%)
  starting transfers between devices  4.17 us (2%)
    reduce_scatter x1, waiting for transfers between devices, shards_general(): lax.psum_scatter(base_rows, 'tensor', scatter_dimension=2, tiled=True)  47 us
    unnamed x5, waiting for transfers between devices  42.8 us
    psum x1, waiting for transfers between devices, shards_general(): shrink = lax.psum(shrink_part.astype(jnp.bfloat16), 'tensor')  19.6 us
    dot_general x1, matrix products, shards_general(): jnp.einsum('srd,do->sro', hidden, projection_weight, preferred_element_ty...  8.51 us
    all_to_all x2, local copies, waits for them, and re-layouts, shards_general(): lax.all_to_all(base_part, 'batch', split_axis=1, concat_axis=2, tiled=True)  7.52 us
    gather x1, local copies, waits for them, and re-layouts, shards_general(): down = jnp.take(adapter_down_rows, local, axis=0)  6.84 us
    gather x1, local copies, waits for them, and re-layouts, shards_general(): up = jnp.take(adapter_up_rows, local, axis=0)  6.21 us
    all_gather x1, blocking collectives, shards_general(): segments = lax.all_gather(segment_index_rows, 'batch', axis=1, tiled=True)  5.07 us
  transfers between devices with their start and end apart: 5, of which 3 were waited for; matrix products, arithmetic and copies ran while one was open for 22% of the time, Pallas kernels for 0%

commit v1 on v0

--- a/solution.py
+++ b/solution.py
@@ -1,9 +1,13 @@
 import jax
 import jax.numpy as jnp
 from jax import lax
+from jax.experimental import pallas as pl
+from jax.experimental.pallas import tpu as pltpu
 from jax.sharding import PartitionSpec as P
 
 CAP = 2
+SIDE = 4
+MESH = pl.DeviceIdType.MESH
 
 
 def owned_slots(segment_adapter, adapter_row_map, stored_count, own_index):
@@ -55,6 +59,394 @@
     return (base.astype(jnp.float32) + term.astype(jnp.float32)).astype(jnp.bfloat16)
 
 
+def fused_kernel(
+    table_ref,
+    map_ref,
+    seg_ref,
+    hid_ref,
+    w_ref,
+    down_ref,
+    up_ref,
+    out_ref,
+    hid,
+    w_v,
+    down_v,
+    up_v,
+    seg_v,
+    pieces,
+    rows,
+    z_down,
+    z_up,
+    sh_own,
+    sh_recv,
+    term,
+    pass_in,
+    mine_in,
+    far_in,
+    acc,
+    load_sem,
+    seg_send,
+    seg_recv,
+    hid_send,
+    hid_recv,
+    row_send,
+    row_recv,
+    z_send,
+    zd_recv,
+    zu_recv,
+    sh_send,
+    sh_recv_sem,
+    term_send,
+    term_recv,
+):
+    steps, req, width = hid_ref.shape
+    stored, rank, out_width = up_ref.shape
+    columns = w_ref.shape[1]
+    t = lax.axis_index("tensor")
+    b = lax.axis_index("batch")
+    twin = b + 1 - 2 * (b % 2)
+    across = (b + 2) % SIDE
+    far = 3 - b
+    order = (b, twin, across, far)
+
+    def remote(src, dst, send, recv, **where):
+        return pltpu.make_async_remote_copy(
+            src_ref=src,
+            dst_ref=dst,
+            send_sem=send,
+            recv_sem=recv,
+            device_id=where,
+            device_id_type=MESH,
+        )
+
+    own_load = [
+        pltpu.make_async_copy(hid_ref.at[s], hid.at[s, b], load_sem.at[3 + s])
+        for s in range(steps)
+    ]
+    w_load = pltpu.make_async_copy(w_ref, w_v, load_sem.at[0])
+    down_load = pltpu.make_async_copy(down_ref, down_v, load_sem.at[1])
+    up_load = pltpu.make_async_copy(up_ref, up_v, load_sem.at[2])
+    for copy in own_load:
+        copy.start()
+    w_load.start()
+    down_load.start()
+    up_load.start()
+    seg_v[b] = jnp.zeros(seg_v.shape[1:], jnp.int32)
+    for s in range(steps):
+        seg_v[b, s : s + 1, 0:req] = seg_ref[s]
+
+    barrier = pltpu.get_barrier_semaphore()
+    for k in range(1, SIDE):
+        pl.semaphore_signal(
+            barrier, inc=1, device_id={"batch": (b + k) % SIDE}, device_id_type=MESH
+        )
+        pl.semaphore_signal(
+            barrier, inc=1, device_id={"tensor": (t + k) % SIDE}, device_id_type=MESH
+        )
+    pl.semaphore_wait(barrier, 2 * (SIDE - 1))
+
+    sent = []
+
+    def go(copy):
+        copy.start()
+        sent.append(copy)
+
+    def hid_copy(s, kind, src, index, to):
+        return remote(
+            src, hid.at[s, index], hid_send.at[s, kind], hid_recv.at[s, index], batch=to
+        )
+
+    for s in range(steps):
+        go(hid_copy(s, 0, hid_ref.at[s], b, across))
+    for s in range(steps):
+        go(hid_copy(s, 1, hid_ref.at[s], b, twin))
+    for k in range(1, SIDE):
+        go(remote(seg_v.at[b], seg_v.at[b], seg_send.at[k], seg_recv.at[b], batch=order[k]))
+
+    def slots(s, other):
+        first_slot, first_row = jnp.int32(-1), jnp.int32(0)
+        last_slot, last_row = jnp.int32(-1), jnp.int32(0)
+        for j in range(table_ref.shape[2]):
+            position = map_ref[table_ref[s, other, j]]
+            held = position // stored == b
+            row = position % stored
+            first = held & (first_slot < 0)
+            last_slot = jnp.where(held, j, last_slot)
+            last_row = jnp.where(held, row, last_row)
+            first_row = jnp.where(first, row, first_row)
+            first_slot = jnp.where(first, j, first_slot)
+        return first_slot, first_row, last_slot, last_row
+
+    tile = min(512, columns)
+
+    def base(s):
+        @pl.loop(0, columns // tile)
+        def _(i):
+            span = pl.ds(pl.multiple_of(i * tile, tile), tile)
+            value = jnp.dot(
+                hid[s].reshape(SIDE * req, width),
+                w_v[:, span],
+                preferred_element_type=jnp.float32,
+            )
+            pieces[s, :, :, span] = value.astype(jnp.bfloat16).reshape(SIDE, req, tile)
+
+    def shrink(s):
+        @pl.loop(0, SIDE)
+        def _(other):
+            first_slot, first_row, last_slot, last_row = slots(s, other)
+            factors = jnp.concatenate([down_v[first_row], down_v[last_row]], axis=0)
+            value = lax.dot_general(
+                hid[s, other],
+                factors,
+                (((1,), (1,)), ((), ())),
+                preferred_element_type=jnp.float32,
+            )
+            line = seg_v[other, s : s + 1, 0:req].astype(jnp.float32)
+            diagonal = lax.broadcasted_iota(
+                jnp.int32, (req, req), 0
+            ) == lax.broadcasted_iota(jnp.int32, (req, req), 1)
+            segment = jnp.sum(
+                jnp.where(diagonal, jnp.broadcast_to(line, (req, req)), 0.0),
+                axis=1,
+                keepdims=True,
+            )
+            lane = lax.broadcasted_iota(jnp.int32, (req, CAP * rank), 1)
+            wanted = jnp.where(lane < rank, first_slot, last_slot).astype(jnp.float32)
+            sh_own[s, other] = jnp.where(segment == wanted, value, 0.0).astype(jnp.bfloat16)
+
+        for k in range(1, SIDE):
+            to = (t + k) % SIDE
+            go(
+                remote(
+                    sh_own.at[s],
+                    sh_recv.at[s, k - 1],
+                    sh_send.at[s, k - 1],
+                    sh_recv_sem.at[s, k - 1],
+                    tensor=to,
+                )
+            )
+
+    def row_copy(s, k, index):
+        return remote(
+            pieces.at[s, order[k]],
+            rows.at[s, index],
+            row_send.at[s, k],
+            row_recv.at[s, index],
+            batch=order[k],
+        )
+
+    for s in range(steps):
+        hid_copy(s, 0, hid_ref.at[s], across, across).wait_recv()
+        go(hid_copy(s, 2, hid.at[s, across], across, twin))
+        own_load[s].wait()
+        hid_copy(s, 1, hid_ref.at[s], twin, twin).wait_recv()
+        hid_copy(s, 2, hid.at[s, far], far, twin).wait_recv()
+        if s == 0:
+            w_load.wait()
+        base(s)
+        for k in (2, 3, 1):
+            go(row_copy(s, k, b))
+        rows[s, b] = pieces[s, b]
+        if s == 0:
+            down_load.wait()
+            for k in range(1, SIDE):
+                remote(
+                    seg_v.at[b], seg_v.at[order[k]], seg_send.at[k], seg_recv.at[order[k]],
+                    batch=order[k],
+                ).wait_recv()
+        shrink(s)
+
+    term_tile = min(512, out_width)
+
+    def term_copy(s, kind, src, dst, to):
+        return remote(src, dst, term_send.at[s, kind], term_recv.at[s, kind], batch=to)
+
+    def terms(s):
+        for k in range(SIDE - 1):
+            remote(
+                sh_own.at[s],
+                sh_recv.at[s, k],
+                sh_send.at[s, k],
+                sh_recv_sem.at[s, k],
+                tensor=(t + 1) % SIDE,
+            ).wait_recv()
+        if s == 0:
+            up_load.wait()
+
+        @pl.loop(0, SIDE)
+        def _(other):
+            _, first_row, _, last_row = slots(s, other)
+            total = sh_own[s, other].astype(jnp.float32)
+            for k in range(SIDE - 1):
+                total = total + sh_recv[s, k, other].astype(jnp.float32)
+            masked = total.astype(jnp.bfloat16)
+            for i in range(out_width // term_tile):
+                span = pl.ds(i * term_tile, term_tile)
+                factors = jnp.concatenate(
+                    [up_v[first_row, :, span], up_v[last_row, :, span]], axis=0
+                )
+                term[s, other, :, span] = jnp.dot(
+                    masked, factors, preferred_element_type=jnp.float32
+                ).astype(jnp.bfloat16)
+
+        go(term_copy(s, 0, term.at[s, far], pass_in.at[s], twin))
+        go(term_copy(s, 1, term.at[s, twin], mine_in.at[s], twin))
+
+    def terms_across(s):
+        term_copy(s, 0, term.at[s, far], pass_in.at[s], twin).wait_recv()
+        term[s, across] = term[s, across] + pass_in[s]
+        go(term_copy(s, 2, term.at[s, across], far_in.at[s], across))
+
+    def z_copy(s, c, up):
+        return remote(
+            rows.at[s, c],
+            (z_up if up else z_down).at[s, c],
+            z_send.at[s, c],
+            (zu_recv if up else zd_recv).at[s, c],
+            tensor=(t + 1) % SIDE if up else (t + SIDE - 1) % SIDE,
+        )
+
+    def z_item(s, k):
+        c = order[k]
+        if k:
+            row_copy(s, k, c).wait_recv()
+        for up in (False, True):
+            moves = t < c if up else t > c
+            inner = t > 0 if up else t < SIDE - 1
+
+            @pl.when(moves & inner)
+            def _():
+                remote(
+                    rows.at[s, c],
+                    (z_up if up else z_down).at[s, c],
+                    z_send.at[s, c],
+                    (zu_recv if up else zd_recv).at[s, c],
+                    tensor=(t + 1) % SIDE,
+                ).wait_recv()
+                got = (z_up if up else z_down)[s, c].astype(jnp.float32)
+                rows[s, c] = (rows[s, c].astype(jnp.float32) + got).astype(jnp.bfloat16)
+
+            @pl.when(moves)
+            def _():
+                z_copy(s, c, up).start()
+
+    z_item(0, 0)
+    z_item(0, 1)
+    terms(0)
+    z_item(1, 0)
+    z_item(1, 1)
+    z_item(0, 2)
+    z_item(0, 3)
+    terms(1)
+    terms_across(0)
+    z_item(1, 2)
+    z_item(1, 3)
+    terms_across(1)
+
+    for s in range(steps):
+        term_copy(s, 1, term.at[s, twin], mine_in.at[s], twin).wait_recv()
+        acc[...] = (
+            rows[s, t].astype(jnp.float32)
+            + term[s, b].astype(jnp.float32)
+            + mine_in[s].astype(jnp.float32)
+        )
+        for up in (False, True):
+
+            @pl.when(t > 0 if up else t < SIDE - 1)
+            def _():
+                remote(
+                    rows.at[s, t],
+                    (z_up if up else z_down).at[s, t],
+                    z_send.at[s, t],
+                    (zu_recv if up else zd_recv).at[s, t],
+                    tensor=(t + 1) % SIDE,
+                ).wait_recv()
+                acc[...] += (z_up if up else z_down)[s, t].astype(jnp.float32)
+
+        term_copy(s, 2, term.at[s, across], far_in.at[s], across).wait_recv()
+        out_ref[s] = (acc[...] + far_in[s].astype(jnp.float32)).astype(jnp.bfloat16)
+
+    for copy in sent:
+        copy.wait_send()
+    for s in range(steps):
+        for c in range(SIDE):
+
+            @pl.when(t != c)
+            def _():
+                z_copy(s, c, True).wait_send()
+
+
+def shards_fused(
+    hidden_input,
+    projection_weight,
+    adapter_down_rows,
+    adapter_up_rows,
+    adapter_row_map,
+    segment_index_rows,
+    segment_adapter,
+):
+    steps, req, width = hidden_input.shape
+    columns = projection_weight.shape[1]
+    stored, rank, out_width = adapter_up_rows.shape
+    bf16 = jnp.bfloat16
+    dma = pltpu.SemaphoreType.DMA
+    vmem = pl.BlockSpec(memory_space=pltpu.VMEM)
+    smem = pl.BlockSpec(memory_space=pltpu.SMEM)
+    whole = pl.BlockSpec(memory_space=pl.ANY)
+    block = (steps, SIDE, req, out_width)
+    scratch = [
+        pltpu.VMEM((steps, SIDE, req, width), bf16),
+        pltpu.VMEM(projection_weight.shape, bf16),
+        pltpu.VMEM(adapter_down_rows.shape, bf16),
+        pltpu.VMEM(adapter_up_rows.shape, bf16),
+        pltpu.VMEM((SIDE, 8, 128), jnp.int32),
+        pltpu.VMEM((steps, SIDE, req, columns), bf16),
+        pltpu.VMEM(block, bf16),
+        pltpu.VMEM(block, bf16),
+        pltpu.VMEM(block, bf16),
+        pltpu.VMEM((steps, SIDE, req, CAP * rank), bf16),
+        pltpu.VMEM((steps, SIDE - 1, SIDE, req, CAP * rank), bf16),
+        pltpu.VMEM(block, bf16),
+        pltpu.VMEM((steps, req, out_width), bf16),
+        pltpu.VMEM((steps, req, out_width), bf16),
+        pltpu.VMEM((steps, req, out_width), bf16),
+        pltpu.VMEM((req, out_width), jnp.float32),
+        dma((3 + steps,)),
+        dma((SIDE,)),
+        dma((SIDE,)),
+        dma((steps, 3)),
+        dma((steps, SIDE)),
+        dma((steps, SIDE)),
+        dma((steps, SIDE)),
+        dma((steps, SIDE)),
+        dma((steps, SIDE)),
+        dma((steps, SIDE)),
+        dma((steps, SIDE)),
+        dma((steps, SIDE)),
+        dma((steps, 3)),
+        dma((steps, 3)),
+    ]
+    return pl.pallas_call(
+        fused_kernel,
+        out_shape=jax.ShapeDtypeStruct((steps, req, out_width), bf16),
+        in_specs=[smem, smem, vmem, whole, whole, whole, whole],
+        out_specs=vmem,
+        scratch_shapes=scratch,
+        compiler_params=pltpu.CompilerParams(
+            collective_id=0, has_side_effects=True, vmem_limit_bytes=56 * 1024 * 1024
+        ),
+        name="fused_projection",
+    )(
+        segment_adapter,
+        adapter_row_map,
+        segment_index_rows,
+        hidden_input,
+        projection_weight,
+        adapter_down_rows,
+        adapter_up_rows,
+    )
+
+
 def solution(mesh):
     in_specs = (
         P(None, ("group", "batch"), "tensor"),
@@ -66,6 +458,7 @@
         P(None, "group", None),
     )
     out_specs = P(None, ("group", "batch"), "tensor")
+    fused = mesh.shape["tensor"] == SIDE and mesh.shape["batch"] == SIDE
     return jax.shard_map(
-        shards_general, mesh=mesh, in_specs=in_specs, out_specs=out_specs, check_vma=False
+        shards_fused if fused else shards_general, mesh=mesh, in_specs=in_specs, out_specs=out_specs, check_vma=False
     )

time: 188 us -> 86.4 us (0.46)
  the two profiles are of different devices: /device:TPU:6 before, /device:TPU:23 now
where the time goes in v1:
time: 86.4 us; the launch traced here: 86.2 us
  Pallas kernels  84.3 us (98%)
  local copies, waits for them, and re-layouts  1.88 us (2%)
    pallas_call x1, Pallas kernels, shards_fused(): pl.pallas_call(fused_kernel, out_shape=jax.ShapeDtypeStruct((steps, req,...  84.3 us
    unnamed x1, local copies, waits for them, and re-layouts  1.88 us

profile of v1, /device:TPU:23, one launch (start us, length us, event | category | flops | bytes accessed | tf_op | source)
XLA Modules:
  0.0 86.2 jit_solution(1786402111444169273)
XLA Ops:
  0.0 84.3 %fused_projection.1 = bf16[2,64,2048]{2,1,0:T(8,128)(2,1)} custom-call(s32[2,4,4]{2,1,0:T(4,128)} %table_ref.1, s32[128]{0:T(128)} %map_ref.1, s32[2,1,64]{2,1,0:T(1,128)} %seg_ref.1, bf16[2,64,2048]{2,1,0:T(8,128)(2,1)} %hid_ref.1, bf16[2048,2048]{1,0:T(8,128)(2,1)} %w_ref.1, bf16[32,64,2048]{2,1,0:T(8,128)(2,1)} %down_ref.1, bf16[32,64,2048]{2,1,0:T(8,128)(2,1)} %up_ref.1), custom_call_target="tpu_custom_call" | custom-call | tf_op jit(solution)/shard_map/fused_projection/pallas_call | solution.py:429
  84.3 1.9 %copy.9 = bf16[2,64,2048]{2,1,0:T(8,128)(2,1)} copy(bf16[2,64,2048]{2,1,0:T(8,128)(2,1)} %fused_projection.1) | data formatting | bytes 1048576

commit v2 on v1

--- a/solution.py
+++ b/solution.py
@@ -7,6 +7,7 @@
 
 CAP = 2
 SIDE = 4
+PARTS = 4
 MESH = pl.DeviceIdType.MESH
 
 
@@ -120,7 +121,7 @@
         )
 
     own_load = [
-        pltpu.make_async_copy(hid_ref.at[s], hid.at[s, b], load_sem.at[3 + s])
+        pltpu.make_async_copy(hid_ref.at[s], hid.at[b, s], load_sem.at[3 + s])
         for s in range(steps)
     ]
     w_load = pltpu.make_async_copy(w_ref, w_v, load_sem.at[0])
@@ -129,8 +130,6 @@
     for copy in own_load:
         copy.start()
     w_load.start()
-    down_load.start()
-    up_load.start()
     seg_v[b] = jnp.zeros(seg_v.shape[1:], jnp.int32)
     for s in range(steps):
         seg_v[b, s : s + 1, 0:req] = seg_ref[s]
@@ -153,7 +152,7 @@
 
     def hid_copy(s, kind, src, index, to):
         return remote(
-            src, hid.at[s, index], hid_send.at[s, kind], hid_recv.at[s, index], batch=to
+            src, hid.at[index, s], hid_send.at[s, kind], hid_recv.at[s, index], batch=to
         )
 
     for s in range(steps):
@@ -178,17 +177,30 @@
         return first_slot, first_row, last_slot, last_row
 
     tile = min(512, columns)
-
-    def base(s):
+    near_pair = 2 * (b // 2)
+    far_pair = (near_pair + 2) % SIDE
+
+    def base_near():
         @pl.loop(0, columns // tile)
         def _(i):
             span = pl.ds(pl.multiple_of(i * tile, tile), tile)
             value = jnp.dot(
-                hid[s].reshape(SIDE * req, width),
+                hid[pl.ds(near_pair, 2)].reshape(2 * steps * req, width),
                 w_v[:, span],
                 preferred_element_type=jnp.float32,
-            )
-            pieces[s, :, :, span] = value.astype(jnp.bfloat16).reshape(SIDE, req, tile)
+            ).astype(jnp.bfloat16)
+            pieces[pl.ds(near_pair, 2), :, :, span] = value.reshape(2, steps, req, tile)
+
+    def base_far(s):
+        @pl.loop(0, columns // tile)
+        def _(i):
+            span = pl.ds(pl.multiple_of(i * tile, tile), tile)
+            value = jnp.dot(
+                hid[pl.ds(far_pair, 2), s].reshape(2 * req, width),
+                w_v[:, span],
+                preferred_element_type=jnp.float32,
+            ).astype(jnp.bfloat16)
+            pieces[pl.ds(far_pair, 2), s, :, span] = value.reshape(2, req, tile)
 
     def shrink(s):
         @pl.loop(0, SIDE)
@@ -196,7 +208,7 @@
             first_slot, first_row, last_slot, last_row = slots(s, other)
             factors = jnp.concatenate([down_v[first_row], down_v[last_row]], axis=0)
             value = lax.dot_general(
-                hid[s, other],
+                hid[other, s],
                 factors,
                 (((1,), (1,)), ((), ())),
                 preferred_element_type=jnp.float32,
@@ -226,35 +238,53 @@
                 )
             )
 
-    def row_copy(s, k, index):
+    half = req // PARTS
+
+    def row_copy(s, k, h, index):
+        part = pl.ds(h * half, half)
         return remote(
-            pieces.at[s, order[k]],
-            rows.at[s, index],
-            row_send.at[s, k],
-            row_recv.at[s, index],
+            pieces.at[order[k], s, part],
+            rows.at[s, index, part],
+            row_send.at[s, k, h],
+            row_recv.at[s, index, h],
             batch=order[k],
         )
 
-    for s in range(steps):
-        hid_copy(s, 0, hid_ref.at[s], across, across).wait_recv()
-        go(hid_copy(s, 2, hid.at[s, across], across, twin))
-        own_load[s].wait()
-        hid_copy(s, 1, hid_ref.at[s], twin, twin).wait_recv()
-        hid_copy(s, 2, hid.at[s, far], far, twin).wait_recv()
-        if s == 0:
-            w_load.wait()
-        base(s)
-        for k in (2, 3, 1):
-            go(row_copy(s, k, b))
-        rows[s, b] = pieces[s, b]
-        if s == 0:
-            down_load.wait()
-            for k in range(1, SIDE):
-                remote(
-                    seg_v.at[b], seg_v.at[order[k]], seg_send.at[k], seg_recv.at[order[k]],
-                    batch=order[k],
-                ).wait_recv()
-        shrink(s)
+    def z_part(s, c, h, up):
+        part = pl.ds(h * half, half)
+        return remote(
+            rows.at[s, c, part],
+            (z_up if up else z_down).at[s, c, part],
+            z_send.at[s, c, h],
+            (zu_recv if up else zd_recv).at[s, c, h],
+            tensor=(t + 1) % SIDE if up else (t + SIDE - 1) % SIDE,
+        )
+
+    def z_begin(s, k):
+        c = order[k]
+        for h in range(PARTS):
+            if k:
+                row_copy(s, k, h, c).wait_recv()
+            for up in (False, True):
+
+                @pl.when((t == 0) & (c > 0) if up else (t == SIDE - 1) & (c < SIDE - 1))
+                def _():
+                    z_part(s, c, h, up).start()
+
+    def z_relay(s, k):
+        c = order[k]
+        for h in range(PARTS):
+            part = pl.ds(h * half, half)
+            for up in (False, True):
+                inner = (t > 0) & (t < c) if up else (t < SIDE - 1) & (t > c)
+
+                @pl.when(inner)
+                def _():
+                    z_part(s, c, h, up).wait_recv()
+                    got = (z_up if up else z_down)[s, c, part].astype(jnp.float32)
+                    total = rows[s, c, part].astype(jnp.float32) + got
+                    rows[s, c, part] = total.astype(jnp.bfloat16)
+                    z_part(s, c, h, up).start()
 
     term_tile = min(512, out_width)
 
@@ -297,51 +327,56 @@
         term[s, across] = term[s, across] + pass_in[s]
         go(term_copy(s, 2, term.at[s, across], far_in.at[s], across))
 
-    def z_copy(s, c, up):
-        return remote(
-            rows.at[s, c],
-            (z_up if up else z_down).at[s, c],
-            z_send.at[s, c],
-            (zu_recv if up else zd_recv).at[s, c],
-            tensor=(t + 1) % SIDE if up else (t + SIDE - 1) % SIDE,
-        )
-
-    def z_item(s, k):
-        c = order[k]
-        if k:
-            row_copy(s, k, c).wait_recv()
-        for up in (False, True):
-            moves = t < c if up else t > c
-            inner = t > 0 if up else t < SIDE - 1
-
-            @pl.when(moves & inner)
-            def _():
-                remote(
-                    rows.at[s, c],
-                    (z_up if up else z_down).at[s, c],
-                    z_send.at[s, c],
-                    (zu_recv if up else zd_recv).at[s, c],
-                    tensor=(t + 1) % SIDE,
-                ).wait_recv()
-                got = (z_up if up else z_down)[s, c].astype(jnp.float32)
-                rows[s, c] = (rows[s, c].astype(jnp.float32) + got).astype(jnp.bfloat16)
-
-            @pl.when(moves)
-            def _():
-                z_copy(s, c, up).start()
-
-    z_item(0, 0)
-    z_item(0, 1)
+    for s in range(steps):
+        own_load[s].wait()
+        hid_copy(s, 1, hid_ref.at[s], twin, twin).wait_recv()
+    w_load.wait()
+    down_load.start()
+    up_load.start()
+    base_near()
+    for s in range(steps):
+        for h in range(PARTS):
+            go(row_copy(s, 1, h, b))
+        rows[s, b] = pieces[b, s]
+    z_begin(0, 0)
+
+    def far_half(s):
+        hid_copy(s, 0, hid_ref.at[s], across, across).wait_recv()
+        go(hid_copy(s, 2, hid.at[across, s], across, twin))
+        hid_copy(s, 2, hid.at[far, s], far, twin).wait_recv()
+        base_far(s)
+        for k in (2, 3):
+            for h in range(PARTS):
+                go(row_copy(s, k, h, b))
+
+    far_half(0)
+    down_load.wait()
+    for k in range(1, SIDE):
+        remote(
+            seg_v.at[b], seg_v.at[order[k]], seg_send.at[k], seg_recv.at[order[k]], batch=order[k]
+        ).wait_recv()
+    shrink(0)
+    z_begin(0, 1)
+    far_half(1)
+    shrink(1)
+    z_begin(1, 0)
+    z_begin(1, 1)
+    z_relay(0, 0)
+    z_begin(0, 2)
     terms(0)
-    z_item(1, 0)
-    z_item(1, 1)
-    z_item(0, 2)
-    z_item(0, 3)
+    z_relay(0, 1)
+    terms_across(0)
     terms(1)
-    terms_across(0)
-    z_item(1, 2)
-    z_item(1, 3)
+    z_relay(0, 2)
+    z_begin(0, 3)
     terms_across(1)
+    z_relay(1, 0)
+    z_relay(0, 3)
+    z_begin(1, 2)
+    z_relay(1, 1)
+    z_begin(1, 3)
+    z_relay(1, 2)
+    z_relay(1, 3)
 
     for s in range(steps):
         term_copy(s, 1, term.at[s, twin], mine_in.at[s], twin).wait_recv()
@@ -354,13 +389,8 @@
 
             @pl.when(t > 0 if up else t < SIDE - 1)
             def _():
-                remote(
-                    rows.at[s, t],
-                    (z_up if up else z_down).at[s, t],
-                    z_send.at[s, t],
-                    (zu_recv if up else zd_recv).at[s, t],
-                    tensor=(t + 1) % SIDE,
-                ).wait_recv()
+                for h in range(PARTS):
+                    z_part(s, t, h, up).wait_recv()
                 acc[...] += (z_up if up else z_down)[s, t].astype(jnp.float32)
 
         term_copy(s, 2, term.at[s, across], far_in.at[s], across).wait_recv()
@@ -370,10 +400,11 @@
         copy.wait_send()
     for s in range(steps):
         for c in range(SIDE):
-
-            @pl.when(t != c)
-            def _():
-                z_copy(s, c, True).wait_send()
+            for h in range(PARTS):
+
+                @pl.when(t != c)
+                def _():
+                    z_part(s, c, h, True).wait_send()
 
 
 def shards_fused(
@@ -395,12 +426,12 @@
     whole = pl.BlockSpec(memory_space=pl.ANY)
     block = (steps, SIDE, req, out_width)
     scratch = [
-        pltpu.VMEM((steps, SIDE, req, width), bf16),
+        pltpu.VMEM((SIDE, steps, req, width), bf16),
         pltpu.VMEM(projection_weight.shape, bf16),
         pltpu.VMEM(adapter_down_rows.shape, bf16),
         pltpu.VMEM(adapter_up_rows.shape, bf16),
         pltpu.VMEM((SIDE, 8, 128), jnp.int32),
-        pltpu.VMEM((steps, SIDE, req, columns), bf16),
+        pltpu.VMEM((SIDE, steps, req, columns), bf16),
         pltpu.VMEM(block, bf16),
         pltpu.VMEM(block, bf16),
         pltpu.VMEM(block, bf16),
@@ -416,11 +447,11 @@
         dma((SIDE,)),
         dma((steps, 3)),
         dma((steps, SIDE)),
-        dma((steps, SIDE)),
-        dma((steps, SIDE)),
-        dma((steps, SIDE)),
-        dma((steps, SIDE)),
-        dma((steps, SIDE)),
+        dma((steps, SIDE, PARTS)),
+        dma((steps, SIDE, PARTS)),
+        dma((steps, SIDE, PARTS)),
+        dma((steps, SIDE, PARTS)),
+        dma((steps, SIDE, PARTS)),
         dma((steps, SIDE)),
         dma((steps, SIDE)),
         dma((steps, 3)),

time: 86.4 us -> 76.3 us (0.88)
  the two profiles are of different devices: /device:TPU:23 before, /device:TPU:6 now
where the time goes in v2:
time: 76.3 us; the launch traced here: 76.1 us
  Pallas kernels  74.2 us (97%)
  local copies, waits for them, and re-layouts  1.88 us (2%)
    pallas_call x1, Pallas kernels, shards_fused(): pl.pallas_call(fused_kernel, out_shape=jax.ShapeDtypeStruct((steps, req,...  74.2 us
    unnamed x1, local copies, waits for them, and re-layouts  1.88 us

profile of v2, /device:TPU:6, one launch (start us, length us, event | category | flops | bytes accessed | tf_op | source)
XLA Modules:
  0.0 76.1 jit_solution(2549382264909290086)
XLA Ops:
  0.0 74.2 %fused_projection.1 = bf16[2,64,2048]{2,1,0:T(8,128)(2,1)} custom-call(s32[2,4,4]{2,1,0:T(4,128)} %table_ref.1, s32[128]{0:T(128)} %map_ref.1, s32[2,1,64]{2,1,0:T(1,128)} %seg_ref.1, bf16[2,64,2048]{2,1,0:T(8,128)(2,1)} %hid_ref.1, bf16[2048,2048]{1,0:T(8,128)(2,1)} %w_ref.1, bf16[32,64,2048]{2,1,0:T(8,128)(2,1)} %down_ref.1, bf16[32,64,2048]{2,1,0:T(8,128)(2,1)} %up_ref.1), custom_call_target="tpu_custom_call" | custom-call | tf_op jit(solution)/shard_map/fused_projection/pallas_call | solution.py:460
  74.2 1.9 %copy.9 = bf16[2,64,2048]{2,1,0:T(8,128)(2,1)} copy(bf16[2,64,2048]{2,1,0:T(8,128)(2,1)} %fused_projection.1) | data formatting | bytes 1048576

commit v3 on v2

--- a/solution.py
+++ b/solution.py
@@ -7,7 +7,7 @@
 
 CAP = 2
 SIDE = 4
-PARTS = 4
+PARTS = 2
 MESH = pl.DeviceIdType.MESH
 
 

time: 76.3 us -> 74.8 us (0.980)
  Pallas kernels: 74.2 us -> 72.7 us
    pallas_call x1, Pallas kernels: 74.2 us -> 72.7 us  [shards_fused(): pl.pallas_call(fused_kernel, out_shape=jax.ShapeDtypeStruct((steps, req,...]
where the time goes in v3:
time: 74.8 us; the launch traced here: 74.6 us
  Pallas kernels  72.7 us (97%)
  local copies, waits for them, and re-layouts  1.88 us (3%)
    pallas_call x1, Pallas kernels, shards_fused(): pl.pallas_call(fused_kernel, out_shape=jax.ShapeDtypeStruct((steps, req,...  72.7 us
    unnamed x1, local copies, waits for them, and re-layouts  1.88 us

profile of v3, /device:TPU:6, one launch (start us, length us, event | category | flops | bytes accessed | tf_op | source)
XLA Modules:
  0.0 74.6 jit_solution(17023874100581903365)
XLA Ops:
  0.0 72.7 %fused_projection.1 = bf16[2,64,2048]{2,1,0:T(8,128)(2,1)} custom-call(s32[2,4,4]{2,1,0:T(4,128)} %table_ref.1, s32[128]{0:T(128)} %map_ref.1, s32[2,1,64]{2,1,0:T(1,128)} %seg_ref.1, bf16[2,64,2048]{2,1,0:T(8,128)(2,1)} %hid_ref.1, bf16[2048,2048]{1,0:T(8,128)(2,1)} %w_ref.1, bf16[32,64,2048]{2,1,0:T(8,128)(2,1)} %down_ref.1, bf16[32,64,2048]{2,1,0:T(8,128)(2,1)} %up_ref.1), custom_call_target="tpu_custom_call" | custom-call | tf_op jit(solution)/shard_map/fused_projection/pallas_call | solution.py:460
  72.7 1.9 %copy.9 = bf16[2,64,2048]{2,1,0:T(8,128)(2,1)} copy(bf16[2,64,2048]{2,1,0:T(8,128)(2,1)} %fused_projection.1) | data formatting | bytes 1048576
